TPU v7x, 512 devices: a whole 4x8x8 slice. The times are simulated.
512 devices in a mesh: gx: 4 (over z_lo, core), gy: 32 (over z_hi, y), gz: 4 (over x).
Axes of the slice: x: 4, y: 8, z: 8 (z_hi: 4, z_lo: 2; z = z_hi * 2 + z_lo), core: 2. Of those that a mesh axis runs over, the one named last changes fastest.
Arguments:
- cell_state: float32 [3, 32, 512, 512], P(None, 'gx', 'gy', 'gz'), may hold values from 0 to 1, as said below
- old_mass: float32 [3, 32, 512, 512], P(None, 'gx', 'gy', 'gz'), may hold values from 0 to 1.5
- pore_volume: float32 [32, 512, 512], P('gx', 'gy', 'gz'), may hold values from 0.5 to 2
- transmissibility: float32 [13, 32, 512, 512], P(None, 'gx', 'gy', 'gz'), may hold values from 0.02 to 1
- active_mask: int32 [32, 512, 512], P('gx', 'gy', 'gz'), may hold values 0 or 1
- pvt_region: int32 [32, 512, 512], P('gx', 'gy', 'gz'), may hold values from 0 to 7
- formation_factor: float32 [3, 8], replicated, may hold values from 0.6 to 1.5
- compressibility: float32 [3, 8], replicated, may hold values from 0.05 to 0.2
- inverse_viscosity: float32 [3, 8], replicated, may hold values from 0.3 to 3
Outputs:
- residual: float32 [3, 32, 512, 512], P(None, 'gx', 'gy', 'gz')
- pressure_update: float32 [32, 512, 512], P('gx', 'gy', 'gz')
Inputs may be any that keep to these rules, and one draw needn't show every extreme that they name: `cell_state`: channel 0 is the pressure; channels 1 and 2 are positive saturations whose sum stays below 1.
All inputs are finite; a program needn't handle non-finite values. No bound on the sum of `active_mask` on one device may be relied on, other than what follows from the above.
Results may differ from a plain program's by a relative error of at most 0.0003.
Values sent between devices are 32-bit elements; how exact they have to be, the bound alone decides.
A program may use at most 64 MiB of HBM per device.

v0:
```python
import jax
import jax.numpy as jnp
from jax import lax
from jax.sharding import PartitionSpec as P

SWEEPS = 4


neighbour_offsets = [
    (along_x, along_y, along_z)
    for along_x in (-1, 0, 1)
    for along_y in (-1, 0, 1)
    for along_z in (-1, 0, 1)
    if (along_x, along_y, along_z) != (0, 0, 0)
]
upper_offsets = [offset for offset in neighbour_offsets if offset > (0, 0, 0)]
relax_weight = 0.7


def extended(cells, sides, width):
    for axis, dim in sides:
        count = lax.axis_size(axis)
        ends = count - 1
        head = lax.slice_in_dim(cells, 0, width, axis=dim)
        tail = lax.slice_in_dim(cells, cells.shape[dim] - width, cells.shape[dim], axis=dim)
        cells = jnp.concatenate(
            [
                lax.ppermute(tail, axis, [(i, (i + 1) % count) for i in range(ends)]),
                cells,
                lax.ppermute(head, axis, [((i + 1) % count, i) for i in range(ends)]),
            ],
            axis=dim,
        )
    return cells


def window(values_in, offset):
    extent = values_in.shape[-3:]
    return values_in[
        ...,
        1 + offset[0] : extent[0] - 1 + offset[0],
        1 + offset[1] : extent[1] - 1 + offset[1],
        1 + offset[2] : extent[2] - 1 + offset[2],
    ]


def lookup(table_in, region_float):
    looked_up = jnp.zeros((table_in.shape[0],) + region_float.shape, region_float.dtype)
    for level in range(table_in.shape[1]):
        chosen = (region_float == level).astype(region_float.dtype)
        looked_up = looked_up + table_in[:, level][:, None, None, None] * chosen[None]
    return looked_up


def assemble(padded, old_mass, pore_volume, tables):
    formation, compress_table, viscous_inverse = tables
    pressure = padded[0]
    active = padded[3]
    saturation = jnp.stack([padded[1], 1.0 - padded[1] - padded[2], padded[2]])
    compress_rate = lookup(compress_table, padded[4])
    expansion = lookup(formation, padded[4]) * jnp.exp(compress_rate * (pressure[None] - 0.5))
    mobility = lookup(viscous_inverse, padded[4]) * expansion * saturation * saturation
    slope_all = compress_rate * mobility
    centre = (0, 0, 0)
    press_here = window(pressure, centre)
    active_here = window(active, centre)
    mobility_here = window(mobility, centre)
    slope_here = window(slope_all, centre)
    saturation_here = window(saturation, centre)
    expansion_here = window(expansion, centre)
    storage = pore_volume * jnp.sum(window(compress_rate, centre) * saturation_here, axis=0)
    scaling = 1.0 / jnp.where(active_here > 0, storage, 1.0)
    weights = scaling[None] / expansion_here
    flux_total = jnp.zeros_like(saturation_here)
    diagonal = jnp.ones_like(press_here)
    couplings = []
    for offset in neighbour_offsets:
        if offset in upper_offsets:
            link_trans = window(padded[5 + upper_offsets.index(offset)], centre)
        else:
            mirror = (-offset[0], -offset[1], -offset[2])
            link_trans = window(padded[5 + upper_offsets.index(mirror)], offset)
        link_trans = link_trans * active_here * window(active, offset)
        press_drop = press_here - window(pressure, offset)
        mobility_mean = 0.5 * (mobility_here + window(mobility, offset))
        flux_total = flux_total + link_trans * mobility_mean * press_drop
        diagonal = diagonal + link_trans * jnp.sum(
            weights * (0.5 * slope_here * press_drop + mobility_mean), axis=0
        )
        couplings.append(
            link_trans
            * jnp.sum(
                weights * (0.5 * window(slope_all, offset) * press_drop - mobility_mean), axis=0
            )
        )
    residual = active_here * (
        pore_volume * expansion_here * saturation_here - old_mass + flux_total
    )
    pressure_rhs = -jnp.sum(weights * residual, axis=0)
    return (residual, diagonal, jnp.stack(couplings), pressure_rhs)


def relax(padded_update, diagonal, couplings, pressure_rhs):
    centre_update = window(padded_update, (0, 0, 0))
    product = diagonal * centre_update
    for position, offset in enumerate(neighbour_offsets):
        product = product + couplings[position] * window(padded_update, offset)
    return centre_update + relax_weight * (pressure_rhs - product) / diagonal


def body(
    cell_state,
    old_mass,
    pore_volume,
    transmissibility,
    active_mask,
    pvt_region,
    formation_factor,
    compressibility,
    inverse_viscosity,
):
    tables = (formation_factor, compressibility, inverse_viscosity)
    flag_rows = jnp.stack([active_mask.astype(jnp.float32), pvt_region.astype(jnp.float32)])
    stacked = jnp.concatenate([cell_state, flag_rows, transmissibility], axis=0)
    padded = extended(stacked, (("gx", 1), ("gy", 2), ("gz", 3)), 1)
    residual, diagonal, couplings, pressure_rhs = assemble(padded, old_mass, pore_volume, tables)
    update = relax_weight * pressure_rhs / diagonal
    for sweep_index in range(SWEEPS - 1):
        rimmed = extended(update, (("gx", 0), ("gy", 1), ("gz", 2)), 1)
        update = relax(rimmed, diagonal, couplings, pressure_rhs)
    return (residual, update)


def solution(mesh):
    return jax.shard_map(
        body,
        mesh=mesh,
        in_specs=(
            P(None, "gx", "gy", "gz"),
            P(None, "gx", "gy", "gz"),
            P("gx", "gy", "gz"),
            P(None, "gx", "gy", "gz"),
            P("gx", "gy", "gz"),
            P("gx", "gy", "gz"),
            P(),
            P(),
            P(),
        ),
        out_specs=(P(None, "gx", "gy", "gz"), P("gx", "gy", "gz")),
        check_vma=False,
    )
```

profile of v0, /device:TPU:185, one launch (start us, length us, event | category | flops | bytes accessed | tf_op | source)
XLA Modules:
  0.0 161.8 jit_solution(7526457504079228988)
XLA Ops:
  2.6 4.6 %collective-permute-start = (f32[18,1,16,128]{3,2,1,0:T(8,128)S(1)}, f32[18,1,16,128]{3,2,1,0:T(8,128)S(1)}, u32[]{:S(2)}, u32[]{:S(2)}) collective-permute-start(f32[18,1,16,128]{3,2,1,0:T(8,128)S(1)} %get-tuple-element.296), channel_id=1, source_target_pairs={{0,128},{128,256},{256,384},{1,129},{129,257},{257,385},{2,130},{1... | collective-permute-start | bytes 442376 | tf_op jit(solution)/shard_map/ppermute | solution.py:28
  9.3 4.4 %collective-permute-done.1 = f32[18,1,16,128]{3,2,1,0:T(8,128)S(1)} collective-permute-done((f32[18,1,16,128]{3,2,1,0:T(8,128)S(1)}, f32[18,1,16,128]{3,2,1,0:T(8,128)S(1)}, u32[]{:S(2)}, u32[]{:S(2)}) %collective-permute-start.1) | collective-permute-done | bytes 147488 | tf_op jit(solution)/shard_map/ppermute | solution.py:30
  14.8 5.3 %collective-permute-start.2 = (f32[18,10,1,128]{3,2,1,0:T(1,128)S(1)}, f32[18,10,1,128]{3,2,1,0:T(1,128)S(1)}, u32[]{:S(2)}, u32[]{:S(2)}) collective-permute-start(f32[18,10,1,128]{3,2,1,0:T(1,128)S(1)} %get-tuple-element.294), channel_id=1, source_target_pairs={{0,4},{4,8},{8,12},{12,16},{16,20},{20,24},{24,28},{28,32},{32,36}... | collective-permute-start | bytes 276488 | tf_op jit(solution)/shard_map/ppermute | solution.py:28
  23.1 7.0 %collective-permute-done.3 = f32[18,10,1,128]{3,2,1,0:T(1,128)S(1)} collective-permute-done((f32[18,10,1,128]{3,2,1,0:T(1,128)S(1)}, f32[18,10,1,128]{3,2,1,0:T(1,128)S(1)}, u32[]{:S(2)}, u32[]{:S(2)}) %collective-permute-start.3) | collective-permute-done | bytes 92192 | tf_op jit(solution)/shard_map/ppermute | solution.py:30
  33.2 3.4 %copy.24 = f32[18,10,18,1]{2,3,1,0:T(1,128)} copy(f32[18,10,18,1]{3,2,1,0:T(8,128)} %get-tuple-element.272) | data formatting | bytes 25920
  39.6 4.6 %collective-permute-start.4 = (f32[18,10,18,1]{2,3,1,0:T(1,128)}, f32[18,10,18,1]{2,3,1,0:T(1,128)}, u32[]{:S(2)}, u32[]{:S(2)}) collective-permute-start(f32[18,10,18,1]{2,3,1,0:T(1,128)} %copy.24), channel_id=1, source_target_pairs={{0,1},{1,2},{2,3},{4,5},{5,6},{6,7},{8,9},{9,10},{10,11},{12,13},{... | collective-permute-start | bytes 38888 | tf_op jit(solution)/shard_map/ppermute | solution.py:28
  47.6 3.5 %copy.23 = f32[18,10,18,1]{3,2,1,0:T(8,128)} copy(f32[18,10,18,1]{2,3,1,0:T(1,128)} %collective-permute-done.5) | data formatting | bytes 25920 | tf_op jit(solution)/shard_map/ppermute | solution.py:30
  51.1 7.7 %pad_maximum_fusion = f32[18,10,18,130]{3,2,1,0:T(8,128)S(1)} fusion(f32[18,10,18,1]{3,2,1,0:T(8,128)} %copy.23, f32[18,10,1,128]{3,2,1,0:T(1,128)} %copy-done.4, f32[18,1,16,128]{3,2,1,0:T(8,128)} %copy-done.2, f32[13,8,16,128]{3,2,1,0:T(8,128)S(1)} %copy-done, f32[1,8,16,128]{3,2,1,0:T(8,128)S(1)} %get-tuple-element.438, ...), kind=kLoop, calls=%fused_computation | loop fusion | flops 3790800 | bytes 3369600 | tf_op jit(solution)/shard_map/concatenate | solution.py:26
  69.5 4.6 %collective-permute-start.6 = (f32[1,16,128]{2,1,0:T(8,128)S(1)}, f32[1,16,128]{2,1,0:T(8,128)S(1)}, u32[]{:S(2)}, u32[]{:S(2)}) collective-permute-start(f32[1,16,128]{2,1,0:T(8,128)S(1)} %get-tuple-element.436), channel_id=1, source_target_pairs={{0,128},{128,256},{256,384},{1,129},{129,257},{257,385},{2,130},{1... | collective-permute-start | bytes 24584 | tf_op jit(solution)/shard_map/ppermute | solution.py:28
  81.0 3.4 %collective-permute-start.9 = (f32[10,1,128]{2,1,0:T(1,128)S(1)}, f32[10,1,128]{2,1,0:T(1,128)S(1)}, u32[]{:S(2)}, u32[]{:S(2)}) collective-permute-start(f32[10,1,128]{2,1,0:T(1,128)S(1)} %get-tuple-element.431), channel_id=1, source_target_pairs={{4,0},{8,4},{12,8},{16,12},{20,16},{24,20},{28,24},{32,28},{36,32}... | collective-permute-start | bytes 15368 | tf_op jit(solution)/shard_map/ppermute | solution.py:30
  84.4 5.2 %collective-permute-done.9 = f32[10,1,128]{2,1,0:T(1,128)S(1)} collective-permute-done((f32[10,1,128]{2,1,0:T(1,128)S(1)}, f32[10,1,128]{2,1,0:T(1,128)S(1)}, u32[]{:S(2)}, u32[]{:S(2)}) %collective-permute-start.9) | collective-permute-done | bytes 5152 | tf_op jit(solution)/shard_map/ppermute | solution.py:30
  89.7 4.0 %collective-permute-start.10 = (f32[10,18,1]{2,1,0:T(8,128)S(1)}, f32[10,18,1]{2,1,0:T(8,128)S(1)}, u32[]{:S(2)}, u32[]{:S(2)}) collective-permute-start(f32[10,18,1]{2,1,0:T(8,128)S(1)} %get-tuple-element.412), channel_id=1, source_target_pairs={{0,1},{1,2},{2,3},{4,5},{5,6},{6,7},{8,9},{9,10},{10,11},{12,13},{... | collective-permute-start | bytes 2168 | tf_op jit(solution)/shard_map/ppermute | solution.py:28
  96.6 4.4 %collective-permute-done.11 = f32[10,18,1]{2,1,0:T(8,128)S(1)} collective-permute-done((f32[10,18,1]{2,1,0:T(8,128)S(1)}, f32[10,18,1]{2,1,0:T(8,128)S(1)}, u32[]{:S(2)}, u32[]{:S(2)}) %collective-permute-start.11) | collective-permute-done | bytes 752 | tf_op jit(solution)/shard_map/ppermute | solution.py:30
  106.6 3.0 %collective-permute-done.13 = f32[1,16,128]{2,1,0:T(8,128)S(1)} collective-permute-done((f32[1,16,128]{2,1,0:T(8,128)S(1)}, f32[1,16,128]{2,1,0:T(8,128)S(1)}, u32[]{:S(2)}, u32[]{:S(2)}) %collective-permute-start.13) | collective-permute-done | bytes 8224 | tf_op jit(solution)/shard_map/ppermute | solution.py:30
  111.6 3.4 %collective-permute-start.15 = (f32[10,1,128]{2,1,0:T(1,128)S(1)}, f32[10,1,128]{2,1,0:T(1,128)S(1)}, u32[]{:S(2)}, u32[]{:S(2)}) collective-permute-start(f32[10,1,128]{2,1,0:T(1,128)S(1)} %get-tuple-element.427), channel_id=1, source_target_pairs={{4,0},{8,4},{12,8},{16,12},{20,16},{24,20},{28,24},{32,28},{36,32}... | collective-permute-start | bytes 15368 | tf_op jit(solution)/shard_map/ppermute | solution.py:30
  115.0 5.2 %collective-permute-done.15 = f32[10,1,128]{2,1,0:T(1,128)S(1)} collective-permute-done((f32[10,1,128]{2,1,0:T(1,128)S(1)}, f32[10,1,128]{2,1,0:T(1,128)S(1)}, u32[]{:S(2)}, u32[]{:S(2)}) %collective-permute-start.15) | collective-permute-done | bytes 5152 | tf_op jit(solution)/shard_map/ppermute | solution.py:30
  120.3 3.2 %collective-permute-start.16 = (f32[10,18,1]{2,1,0:T(8,128)S(1)}, f32[10,18,1]{2,1,0:T(8,128)S(1)}, u32[]{:S(2)}, u32[]{:S(2)}) collective-permute-start(f32[10,18,1]{2,1,0:T(8,128)S(1)} %get-tuple-element.410), channel_id=1, source_target_pairs={{0,1},{1,2},{2,3},{4,5},{5,6},{6,7},{8,9},{9,10},{10,11},{12,13},{... | collective-permute-start | bytes 2168 | tf_op jit(solution)/shard_map/ppermute | solution.py:28
  126.4 4.1 %collective-permute-done.17 = f32[10,18,1]{2,1,0:T(8,128)S(1)} collective-permute-done((f32[10,18,1]{2,1,0:T(8,128)S(1)}, f32[10,18,1]{2,1,0:T(8,128)S(1)}, u32[]{:S(2)}, u32[]{:S(2)}) %collective-permute-start.17) | collective-permute-done | bytes 752 | tf_op jit(solution)/shard_map/ppermute | solution.py:30
  131.0 3.2 %collective-permute-start.18 = (f32[1,16,128]{2,1,0:T(8,128)S(1)}, f32[1,16,128]{2,1,0:T(8,128)S(1)}, u32[]{:S(2)}, u32[]{:S(2)}) collective-permute-start(f32[1,16,128]{2,1,0:T(8,128)S(1)} %get-tuple-element.432), channel_id=1, source_target_pairs={{0,128},{128,256},{256,384},{1,129},{129,257},{257,385},{2,130},{1... | collective-permute-start | bytes 24584 | tf_op jit(solution)/shard_map/ppermute | solution.py:28
  136.1 3.0 %collective-permute-done.19 = f32[1,16,128]{2,1,0:T(8,128)S(1)} collective-permute-done((f32[1,16,128]{2,1,0:T(8,128)S(1)}, f32[1,16,128]{2,1,0:T(8,128)S(1)}, u32[]{:S(2)}, u32[]{:S(2)}) %collective-permute-start.19) | collective-permute-done | bytes 8224 | tf_op jit(solution)/shard_map/ppermute | solution.py:30
  141.1 3.4 %collective-permute-start.21 = (f32[10,1,128]{2,1,0:T(1,128)S(1)}, f32[10,1,128]{2,1,0:T(1,128)S(1)}, u32[]{:S(2)}, u32[]{:S(2)}) collective-permute-start(f32[10,1,128]{2,1,0:T(1,128)S(1)} %get-tuple-element.423), channel_id=1, source_target_pairs={{4,0},{8,4},{12,8},{16,12},{20,16},{24,20},{28,24},{32,28},{36,32}... | collective-permute-start | bytes 15368 | tf_op jit(solution)/shard_map/ppermute | solution.py:30
  144.5 5.2 %collective-permute-done.21 = f32[10,1,128]{2,1,0:T(1,128)S(1)} collective-permute-done((f32[10,1,128]{2,1,0:T(1,128)S(1)}, f32[10,1,128]{2,1,0:T(1,128)S(1)}, u32[]{:S(2)}, u32[]{:S(2)}) %collective-permute-start.21) | collective-permute-done | bytes 5152 | tf_op jit(solution)/shard_map/ppermute | solution.py:30
  149.8 3.6 %collective-permute-start.22 = (f32[10,18,1]{2,1,0:T(8,128)S(1)}, f32[10,18,1]{2,1,0:T(8,128)S(1)}, u32[]{:S(2)}, u32[]{:S(2)}) collective-permute-start(f32[10,18,1]{2,1,0:T(8,128)S(1)} %get-tuple-element.408), channel_id=1, source_target_pairs={{0,1},{1,2},{2,3},{4,5},{5,6},{6,7},{8,9},{9,10},{10,11},{12,13},{... | collective-permute-start | bytes 2168 | tf_op jit(solution)/shard_map/ppermute | solution.py:28
  156.3 4.4 %collective-permute-done.23 = f32[10,18,1]{2,1,0:T(8,128)S(1)} collective-permute-done((f32[10,18,1]{2,1,0:T(8,128)S(1)}, f32[10,18,1]{2,1,0:T(8,128)S(1)}, u32[]{:S(2)}, u32[]{:S(2)}) %collective-permute-start.23) | collective-permute-done | bytes 752 | tf_op jit(solution)/shard_map/ppermute | solution.py:30
  (142 shorter events, 56.5 us)
Async XLA Ops:
  2.6 6.6 %collective-permute-start = (f32[18,1,16,128]{3,2,1,0:T(8,128)S(1)}, f32[18,1,16,128]{3,2,1,0:T(8,128)S(1)}, u32[]{:S(2)}, u32[]{:S(2)}) collective-permute-start(f32[18,1,16,128]{3,2,1,0:T(8,128)S(1)} %get-tuple-element.296), channel_id=1, source_target_pairs={{0,128},{128,256},{256,384},{1,129},{129,257},{257,385},{2,130},{1... | collective-permute-start | bytes 442376 | tf_op jit(solution)/shard_map/ppermute | solution.py:28
  7.2 6.5 %collective-permute-start.1 = (f32[18,1,16,128]{3,2,1,0:T(8,128)S(1)}, f32[18,1,16,128]{3,2,1,0:T(8,128)S(1)}, u32[]{:S(2)}, u32[]{:S(2)}) collective-permute-start(f32[18,1,16,128]{3,2,1,0:T(8,128)S(1)} %get-tuple-element.297), channel_id=1, source_target_pairs={{128,0},{256,128},{384,256},{129,1},{257,129},{385,257},{130,2},{2... | collective-permute-start | bytes 442376 | tf_op jit(solution)/shard_map/ppermute | solution.py:30
  14.8 8.3 %collective-permute-start.2 = (f32[18,10,1,128]{3,2,1,0:T(1,128)S(1)}, f32[18,10,1,128]{3,2,1,0:T(1,128)S(1)}, u32[]{:S(2)}, u32[]{:S(2)}) collective-permute-start(f32[18,10,1,128]{3,2,1,0:T(1,128)S(1)} %get-tuple-element.294), channel_id=1, source_target_pairs={{0,4},{4,8},{8,12},{12,16},{16,20},{20,24},{24,28},{28,32},{32,36}... | collective-permute-start | bytes 276488 | tf_op jit(solution)/shard_map/ppermute | solution.py:28
  20.1 9.9 %collective-permute-start.3 = (f32[18,10,1,128]{3,2,1,0:T(1,128)S(1)}, f32[18,10,1,128]{3,2,1,0:T(1,128)S(1)}, u32[]{:S(2)}, u32[]{:S(2)}) collective-permute-start(f32[18,10,1,128]{3,2,1,0:T(1,128)S(1)} %get-tuple-element.295), channel_id=1, source_target_pairs={{4,0},{8,4},{12,8},{16,12},{20,16},{24,20},{28,24},{32,28},{36,32}... | collective-permute-start | bytes 276488 | tf_op jit(solution)/shard_map/ppermute | solution.py:30
  38.4 9.3 %collective-permute-start.5 = (f32[18,10,18,1]{2,3,1,0:T(1,128)}, f32[18,10,18,1]{2,3,1,0:T(1,128)}, u32[]{:S(2)}, u32[]{:S(2)}) collective-permute-start(f32[18,10,18,1]{2,3,1,0:T(1,128)} %copy.25), channel_id=1, source_target_pairs={{1,0},{2,1},{3,2},{5,4},{6,5},{7,6},{9,8},{10,9},{11,10},{13,12},{... | collective-permute-start | bytes 38888 | tf_op jit(solution)/shard_map/ppermute | solution.py:30
  39.6 5.9 %collective-permute-start.4 = (f32[18,10,18,1]{2,3,1,0:T(1,128)}, f32[18,10,18,1]{2,3,1,0:T(1,128)}, u32[]{:S(2)}, u32[]{:S(2)}) collective-permute-start(f32[18,10,18,1]{2,3,1,0:T(1,128)} %copy.24), channel_id=1, source_target_pairs={{0,1},{1,2},{2,3},{4,5},{5,6},{6,7},{8,9},{9,10},{10,11},{12,13},{... | collective-permute-start | bytes 38888 | tf_op jit(solution)/shard_map/ppermute | solution.py:28
  69.5 6.5 %collective-permute-start.6 = (f32[1,16,128]{2,1,0:T(8,128)S(1)}, f32[1,16,128]{2,1,0:T(8,128)S(1)}, u32[]{:S(2)}, u32[]{:S(2)}) collective-permute-start(f32[1,16,128]{2,1,0:T(8,128)S(1)} %get-tuple-element.436), channel_id=1, source_target_pairs={{0,128},{128,256},{256,384},{1,129},{129,257},{257,385},{2,130},{1... | collective-permute-start | bytes 24584 | tf_op jit(solution)/shard_map/ppermute | solution.py:28
  74.1 5.0 %collective-permute-start.7 = (f32[1,16,128]{2,1,0:T(8,128)S(1)}, f32[1,16,128]{2,1,0:T(8,128)S(1)}, u32[]{:S(2)}, u32[]{:S(2)}) collective-permute-start(f32[1,16,128]{2,1,0:T(8,128)S(1)} %get-tuple-element.437), channel_id=1, source_target_pairs={{128,0},{256,128},{384,256},{129,1},{257,129},{385,257},{130,2},{2... | collective-permute-start | bytes 24584 | tf_op jit(solution)/shard_map/ppermute | solution.py:30
  79.1 5.3 %collective-permute-start.8 = (f32[10,1,128]{2,1,0:T(1,128)S(1)}, f32[10,1,128]{2,1,0:T(1,128)S(1)}, u32[]{:S(2)}, u32[]{:S(2)}) collective-permute-start(f32[10,1,128]{2,1,0:T(1,128)S(1)} %get-tuple-element.430), channel_id=1, source_target_pairs={{0,4},{4,8},{8,12},{12,16},{16,20},{20,24},{24,28},{28,32},{32,36}... | collective-permute-start | bytes 15368 | tf_op jit(solution)/shard_map/ppermute | solution.py:28
  81.0 8.6 %collective-permute-start.9 = (f32[10,1,128]{2,1,0:T(1,128)S(1)}, f32[10,1,128]{2,1,0:T(1,128)S(1)}, u32[]{:S(2)}, u32[]{:S(2)}) collective-permute-start(f32[10,1,128]{2,1,0:T(1,128)S(1)} %get-tuple-element.431), channel_id=1, source_target_pairs={{4,0},{8,4},{12,8},{16,12},{20,16},{24,20},{28,24},{32,28},{36,32}... | collective-permute-start | bytes 15368 | tf_op jit(solution)/shard_map/ppermute | solution.py:30
  89.7 6.9 %collective-permute-start.10 = (f32[10,18,1]{2,1,0:T(8,128)S(1)}, f32[10,18,1]{2,1,0:T(8,128)S(1)}, u32[]{:S(2)}, u32[]{:S(2)}) collective-permute-start(f32[10,18,1]{2,1,0:T(8,128)S(1)} %get-tuple-element.412), channel_id=1, source_target_pairs={{0,1},{1,2},{2,3},{4,5},{5,6},{6,7},{8,9},{9,10},{10,11},{12,13},{... | collective-permute-start | bytes 2168 | tf_op jit(solution)/shard_map/ppermute | solution.py:28
  93.8 7.2 %collective-permute-start.11 = (f32[10,18,1]{2,1,0:T(8,128)S(1)}, f32[10,18,1]{2,1,0:T(8,128)S(1)}, u32[]{:S(2)}, u32[]{:S(2)}) collective-permute-start(f32[10,18,1]{2,1,0:T(8,128)S(1)} %get-tuple-element.413), channel_id=1, source_target_pairs={{1,0},{2,1},{3,2},{5,4},{6,5},{7,6},{9,8},{10,9},{11,10},{13,12},{... | collective-permute-start | bytes 2168 | tf_op jit(solution)/shard_map/ppermute | solution.py:30
  101.8 4.9 %collective-permute-start.12 = (f32[1,16,128]{2,1,0:T(8,128)S(1)}, f32[1,16,128]{2,1,0:T(8,128)S(1)}, u32[]{:S(2)}, u32[]{:S(2)}) collective-permute-start(f32[1,16,128]{2,1,0:T(8,128)S(1)} %get-tuple-element.434), channel_id=1, source_target_pairs={{0,128},{128,256},{256,384},{1,129},{129,257},{257,385},{2,130},{1... | collective-permute-start | bytes 24584 | tf_op jit(solution)/shard_map/ppermute | solution.py:28
  104.7 5.0 %collective-permute-start.13 = (f32[1,16,128]{2,1,0:T(8,128)S(1)}, f32[1,16,128]{2,1,0:T(8,128)S(1)}, u32[]{:S(2)}, u32[]{:S(2)}) collective-permute-start(f32[1,16,128]{2,1,0:T(8,128)S(1)} %get-tuple-element.435), channel_id=1, source_target_pairs={{128,0},{256,128},{384,256},{129,1},{257,129},{385,257},{130,2},{2... | collective-permute-start | bytes 24584 | tf_op jit(solution)/shard_map/ppermute | solution.py:30
  109.7 5.3 %collective-permute-start.14 = (f32[10,1,128]{2,1,0:T(1,128)S(1)}, f32[10,1,128]{2,1,0:T(1,128)S(1)}, u32[]{:S(2)}, u32[]{:S(2)}) collective-permute-start(f32[10,1,128]{2,1,0:T(1,128)S(1)} %get-tuple-element.426), channel_id=1, source_target_pairs={{0,4},{4,8},{8,12},{12,16},{16,20},{20,24},{24,28},{28,32},{32,36}... | collective-permute-start | bytes 15368 | tf_op jit(solution)/shard_map/ppermute | solution.py:28
  111.6 8.6 %collective-permute-start.15 = (f32[10,1,128]{2,1,0:T(1,128)S(1)}, f32[10,1,128]{2,1,0:T(1,128)S(1)}, u32[]{:S(2)}, u32[]{:S(2)}) collective-permute-start(f32[10,1,128]{2,1,0:T(1,128)S(1)} %get-tuple-element.427), channel_id=1, source_target_pairs={{4,0},{8,4},{12,8},{16,12},{20,16},{24,20},{28,24},{32,28},{36,32}... | collective-permute-start | bytes 15368 | tf_op jit(solution)/shard_map/ppermute | solution.py:30
  120.3 6.1 %collective-permute-start.16 = (f32[10,18,1]{2,1,0:T(8,128)S(1)}, f32[10,18,1]{2,1,0:T(8,128)S(1)}, u32[]{:S(2)}, u32[]{:S(2)}) collective-permute-start(f32[10,18,1]{2,1,0:T(8,128)S(1)} %get-tuple-element.410), channel_id=1, source_target_pairs={{0,1},{1,2},{2,3},{4,5},{5,6},{6,7},{8,9},{9,10},{10,11},{12,13},{... | collective-permute-start | bytes 2168 | tf_op jit(solution)/shard_map/ppermute | solution.py:28
  123.5 7.0 %collective-permute-start.17 = (f32[10,18,1]{2,1,0:T(8,128)S(1)}, f32[10,18,1]{2,1,0:T(8,128)S(1)}, u32[]{:S(2)}, u32[]{:S(2)}) collective-permute-start(f32[10,18,1]{2,1,0:T(8,128)S(1)} %get-tuple-element.411), channel_id=1, source_target_pairs={{1,0},{2,1},{3,2},{5,4},{6,5},{7,6},{9,8},{10,9},{11,10},{13,12},{... | collective-permute-start | bytes 2168 | tf_op jit(solution)/shard_map/ppermute | solution.py:30
  131.0 5.1 %collective-permute-start.18 = (f32[1,16,128]{2,1,0:T(8,128)S(1)}, f32[1,16,128]{2,1,0:T(8,128)S(1)}, u32[]{:S(2)}, u32[]{:S(2)}) collective-permute-start(f32[1,16,128]{2,1,0:T(8,128)S(1)} %get-tuple-element.432), channel_id=1, source_target_pairs={{0,128},{128,256},{256,384},{1,129},{129,257},{257,385},{2,130},{1... | collective-permute-start | bytes 24584 | tf_op jit(solution)/shard_map/ppermute | solution.py:28
  134.2 5.0 %collective-permute-start.19 = (f32[1,16,128]{2,1,0:T(8,128)S(1)}, f32[1,16,128]{2,1,0:T(8,128)S(1)}, u32[]{:S(2)}, u32[]{:S(2)}) collective-permute-start(f32[1,16,128]{2,1,0:T(8,128)S(1)} %get-tuple-element.433), channel_id=1, source_target_pairs={{128,0},{256,128},{384,256},{129,1},{257,129},{385,257},{130,2},{2... | collective-permute-start | bytes 24584 | tf_op jit(solution)/shard_map/ppermute | solution.py:30
  139.2 5.3 %collective-permute-start.20 = (f32[10,1,128]{2,1,0:T(1,128)S(1)}, f32[10,1,128]{2,1,0:T(1,128)S(1)}, u32[]{:S(2)}, u32[]{:S(2)}) collective-permute-start(f32[10,1,128]{2,1,0:T(1,128)S(1)} %get-tuple-element.422), channel_id=1, source_target_pairs={{0,4},{4,8},{8,12},{12,16},{16,20},{20,24},{24,28},{28,32},{32,36}... | collective-permute-start | bytes 15368 | tf_op jit(solution)/shard_map/ppermute | solution.py:28
  141.1 8.6 %collective-permute-start.21 = (f32[10,1,128]{2,1,0:T(1,128)S(1)}, f32[10,1,128]{2,1,0:T(1,128)S(1)}, u32[]{:S(2)}, u32[]{:S(2)}) collective-permute-start(f32[10,1,128]{2,1,0:T(1,128)S(1)} %get-tuple-element.423), channel_id=1, source_target_pairs={{4,0},{8,4},{12,8},{16,12},{20,16},{24,20},{28,24},{32,28},{36,32}... | collective-permute-start | bytes 15368 | tf_op jit(solution)/shard_map/ppermute | solution.py:30
  149.8 6.5 %collective-permute-start.22 = (f32[10,18,1]{2,1,0:T(8,128)S(1)}, f32[10,18,1]{2,1,0:T(8,128)S(1)}, u32[]{:S(2)}, u32[]{:S(2)}) collective-permute-start(f32[10,18,1]{2,1,0:T(8,128)S(1)} %get-tuple-element.408), channel_id=1, source_target_pairs={{0,1},{1,2},{2,3},{4,5},{5,6},{6,7},{8,9},{9,10},{10,11},{12,13},{... | collective-permute-start | bytes 2168 | tf_op jit(solution)/shard_map/ppermute | solution.py:28
  153.4 7.2 %collective-permute-start.23 = (f32[10,18,1]{2,1,0:T(8,128)S(1)}, f32[10,18,1]{2,1,0:T(8,128)S(1)}, u32[]{:S(2)}, u32[]{:S(2)}) collective-permute-start(f32[10,18,1]{2,1,0:T(8,128)S(1)} %get-tuple-element.409), channel_id=1, source_target_pairs={{1,0},{2,1},{3,2},{5,4},{6,5},{7,6},{9,8},{10,9},{11,10},{13,12},{... | collective-permute-start | bytes 2168 | tf_op jit(solution)/shard_map/ppermute | solution.py:30
  (31 other events, 137.3 us)
where the time goes:
time: 163 us; the launch traced here: 162 us
  starting transfers between devices  66.9 us (41%)
  waiting for transfers between devices  53.8 us (33%)
  other arithmetic  23.3 us (14%)
  local copies, waits for them, and re-layouts  16.3 us (10%)
    ppermute x12, waiting for transfers between devices, extended(): lax.ppermute(head, axis, [((i + 1) % count, i) for i in range(ends)])  48.9 us
    ppermute x12, starting transfers between devices, extended(): lax.ppermute(tail, axis, [(i, (i + 1) % count) for i in range(ends)])  41.8 us
    ppermute x12, starting transfers between devices, extended(): lax.ppermute(head, axis, [((i + 1) % count, i) for i in range(ends)])  25.1 us
    concatenate x11, other arithmetic, extended(): jnp.concatenate([lax.ppermute(tail, axis, [(i, (i + 1) % count) for i in...  8.74 us
    unnamed x64, local copies, waits for them, and re-layouts  6.45 us
    reduce_sum x8, other arithmetic, assemble(): jnp.sum(weights * (0.5 * window(slope_all, offset) * press_drop - mobilit...  5.3 us
    ppermute x12, waiting for transfers between devices, extended(): lax.ppermute(tail, axis, [(i, (i + 1) % count) for i in range(ends)])  4.85 us
    ppermute x1, local copies, waits for them, and re-layouts, extended(): lax.ppermute(head, axis, [((i + 1) % count, i) for i in range(ends)])  3.45 us
  transfers between devices with their start and end apart: 24, of which 16 were waited for; matrix products, arithmetic and copies ran while one was open for 3% of the time, Pallas kernels for 0%

commit v1 on v0

v1 whole, which is shorter than its diff:
```python
import functools
import itertools

import jax
import jax.numpy as jnp
from jax import lax
from jax.experimental import pallas as pl
from jax.experimental.pallas import tpu as pltpu
from jax.sharding import PartitionSpec as P

MESH = pl.DeviceIdType.MESH
F32 = jnp.float32
AXES = ("gx", "gy", "gz")
relax_weight = 0.7

offsets = [o for o in itertools.product((-1, 0, 1), repeat=3) if o != (0, 0, 0)]
upper = [o for o in offsets if o > (0, 0, 0)]
minus = lambda o: (-o[0], -o[1], -o[2])

OM, PV, PR, SW, SG, AM, RG = 0, 3, 11, 12, 13, 14, 15
TCH = {4: 4, 5: 5, 6: 6, 7: 7, 8: 8, 9: 9, 0: 10, 10: 16, 11: 17, 12: 18, 1: 19, 2: 20, 3: 21}
NCH = 22
X_LOW, X_HIGH = (4, 19), (11, 16)
Y_LOW, Y_LOW2, Y_HIGH = (7, 22), (11, 22), (4, 16)
REST_LOW, REST_HIGH = ((0, 7),), ((0, 4), (16, 22))

NP, NR = 10, 32
T_ROLLED = [k for k, o in enumerate(upper) if o[2] != 0]
PACKED = [PR, SW, SG, AM, RG] + [TCH[k] for k in T_ROLLED]


def rows_sent(dy, wide):
    if dy == 0:
        return (7, 25) if wide else (8, 24), (7, 25) if wide else (8, 24)
    if dy > 0:
        return (22, 24), (6, 8)
    return (8, 10), (24, 26)


def kernel(
    cs, om, pv, tr, am, rg, b_hbm, c_hbm, v_hbm,
    res_out, x_out,
    b_tab, c_tab, v_tab, ext, ints, fld, tl, wts, base, acoef, dinv, xs, px, zx, pk, zb, zf,
    in_sem, s_state, r_state, s_rest, r_rest, s_x, r_x,
):
    me = [lax.axis_index(a) for a in AXES]
    dims = [lax.axis_size(a) for a in AXES]

    def present(o):
        cond = None
        for i, s in enumerate(o):
            if s:
                here = me[i] + s >= 0 if s < 0 else me[i] + s < dims[i]
                cond = here if cond is None else cond & here
        return cond

    def device(o):
        return tuple(jnp.clip(me[i] + s, 0, dims[i] - 1) if s else me[i] for i, s in enumerate(o))

    loads = [
        (cs, ext.at[PR : PR + 3, 1:9, 8:24]),
        (om, ext.at[OM : OM + 3, 1:9, 8:24]),
        (pv, ext.at[PV, 1:9, 8:24]),
        (am, ints.at[0]),
        (rg, ints.at[1]),
        (tr.at[0], ext.at[10, 1:9, 8:24]),
        (tr.at[4:10], ext.at[4:10, 1:9, 8:24]),
        (tr.at[10:13], ext.at[16:19, 1:9, 8:24]),
        (tr.at[1:4], ext.at[19:22, 1:9, 8:24]),
        (b_hbm, b_tab),
        (c_hbm, c_tab),
        (v_hbm, v_tab),
    ]
    copies = [pltpu.make_async_copy(a, b, in_sem.at[i]) for i, (a, b) in enumerate(loads)]
    for c in copies:
        c.start()

    first = [me[i] == 0 for i in range(3)]
    last = [me[i] == dims[i] - 1 for i in range(3)]

    def zero(ref):
        ref[...] = jnp.zeros(ref.shape, ref.dtype)

    @pl.when(first[0])
    def _():
        zero(ext.at[4:19, 0])

    @pl.when(last[0])
    def _():
        zero(ext.at[11:16, 9])

    @pl.when(first[1])
    def _():
        zero(ext.at[:, :, 0:8])

    @pl.when(last[1])
    def _():
        zero(ext.at[:, :, 24:32])

    border = first[0] | first[1] | first[2] | last[0] | last[1] | last[2]

    @pl.when(border)
    def _():
        zero(zb)
        zero(zx)
        for n in range(3):
            zero(xs.at[n, 1])

    barrier = pltpu.get_barrier_semaphore()
    for o in offsets:

        @pl.when(present(o))
        def _(o=o):
            pl.semaphore_signal(barrier, inc=1, device_id=device(o), device_id_type=MESH)

    for c in copies:
        c.wait()

    def convert(i, carry):
        ext[AM, i + 1, 8:24] = ints[0, i].astype(F32)
        ext[RG, i + 1, 8:24] = ints[1, i].astype(F32)
        return carry

    lax.fori_loop(0, 8, convert, 0)

    lane16 = lax.broadcasted_iota(jnp.int32, (16, 128), 1)
    lane24 = lax.broadcasted_iota(jnp.int32, (24, 128), 1)
    even24 = lane24 % 2 == 0

    def pack(x, accs):
        accs = list(accs)
        for s, ch in enumerate(PACKED):
            to = 16 * (s % 8) + 2 * x
            moved = pltpu.roll(ext[ch, x + 1, 8:24], to + 1, 1)
            accs[s // 8] = jnp.where((lane16 == to) | (lane16 == to + 1), moved, accs[s // 8])
        return tuple(accs)

    packed = lax.fori_loop(0, 8, pack, (jnp.zeros((16, 128), F32),) * 2)
    for k in range(2):
        pk[k, 8:24] = packed[k]

    peers = 1
    for i in range(3):
        peers = peers * (1 + (me[i] > 0).astype(jnp.int32) + (me[i] < dims[i] - 1).astype(jnp.int32))
    pl.semaphore_wait(barrier, peers - 1)

    def messages_state():
        found = []
        for dy, (lo, hi), row, to in (
            (1, Y_LOW, 23, 7),
            (-1, Y_HIGH, 8, 24),
            (1, Y_LOW2, 22, 6),
            (-1, Y_HIGH, 9, 25),
        ):
            found.append(((0, dy, 0), ext.at[lo:hi, 1:9, row : row + 1], ext.at[lo:hi, 1:9, to : to + 1]))
        for o in sorted(offsets, key=lambda o: -abs(o[1])):
            dx, dy, dz = o
            (a, b), (c, d) = rows_sent(dy, False)
            if dz:
                side = 0 if dz > 0 else 1
                found.append((o, pk.at[:, a:b], zb.at[side, 1 - dx, :, c:d]))
            elif dx:
                chans = slice(*(X_LOW if dx > 0 else X_HIGH))
                p_from, p_to = (8, 0) if dx > 0 else (1, 9)
                found.append((o, ext.at[chans, p_from, a:b], ext.at[chans, p_to, c:d]))
        return found

    def messages_rest():
        found = []
        for lo, hi in REST_LOW:
            found.append(((0, 1, 0), ext.at[lo:hi, 1:9, 23:24], ext.at[lo:hi, 1:9, 7:8]))
        for lo, hi in REST_HIGH:
            found.append(((0, -1, 0), ext.at[lo:hi, 1:9, 8:9], ext.at[lo:hi, 1:9, 24:25]))
        return found

    def messages_x(n, wide):
        x = xs.at[n, 1]
        found = []
        for o in offsets:
            dx, dy, dz = o
            if wide and dy:
                continue
            (a, b), (c, d) = rows_sent(dy, wide)
            if dz:
                side = 0 if dz > 0 else 1
                found.append((o, px.at[n, a:b], zx.at[n, side, 1 - dx, c:d]))
            elif dx:
                p_from, p_to = (8, 0) if dx > 0 else (1, 9)
                found.append((o, x.at[p_from, a:b], x.at[p_to, c:d]))
            else:
                found.append((o, x.at[1:9, a:b], x.at[1:9, c:d]))
        return found

    def exchange(found, send, recv):
        found = [
            (
                o,
                pltpu.make_async_remote_copy(
                    src_ref=a,
                    dst_ref=b,
                    send_sem=send.at[i],
                    recv_sem=recv.at[i],
                    device_id=device(o),
                    device_id_type=MESH,
                ),
            )
            for i, (o, a, b) in enumerate(found)
        ]

        def start():
            for o, c in found:
                pl.when(present(o))(c.start)

        def arrived():
            for o, c in found:
                pl.when(present(minus(o)))(c.wait_recv)

        def left():
            for o, c in found:
                pl.when(present(o))(c.wait_send)

        return start, arrived, left

    state = exchange(messages_state(), s_state, r_state)
    rest = exchange(messages_rest(), s_rest, r_rest)
    state[0]()
    rest[0]()

    tables = [[[t[c, k] for k in range(8)] for c in range(3)] for t in (b_tab, c_tab, v_tab)]

    def properties(p, sw, sg, m, r):
        b2 = r >= 4.0
        r = jnp.where(b2, r - 4.0, r)
        b1 = r >= 2.0
        b0 = jnp.where(b1, r - 2.0, r) >= 1.0

        def look(t):
            low = jnp.where(b1, jnp.where(b0, t[3], t[2]), jnp.where(b0, t[1], t[0]))
            high = jnp.where(b1, jnp.where(b0, t[7], t[6]), jnp.where(b0, t[5], t[4]))
            return jnp.where(b2, high, low)

        sat = (sw, 1.0 - sw - sg, sg)
        mob, slope, fac = [], [], []
        stored = None
        for c in range(3):
            rate = look(tables[1][c])
            f = look(tables[0][c]) * jnp.exp(rate * (p - 0.5))
            half = 0.5 * look(tables[2][c]) * f * sat[c] * sat[c]
            fac.append(f)
            mob.append(half)
            slope.append(rate * half)
            stored = rate * sat[c] if stored is None else stored + rate * sat[c]
        return [p, m, *mob, *slope], fac, sat, stored

    def across(plane, row):
        return (slice(plane, plane + 8), row)

    def weights(m, vol, old, fac, sat, stored):
        scale = 1.0 / jnp.where(m > 0, vol * stored, 1.0)
        return [scale / f for f in fac], [vol * f * v - o for f, v, o in zip(fac, sat, old)]

    STATE = (PR, SW, SG, AM, RG)

    def fill_own(i, carry):
        at = (i + 1, slice(8, 24))
        fields, fac, sat, stored = properties(*[ext[(ch, *at)] for ch in STATE])
        for f in range(8):
            fld[(1, f, *at)] = fields[f]
        old = [ext[(OM + c, *at)] for c in range(3)]
        ws, bs = weights(fields[1], ext[(PV, *at)], old, fac, sat, stored)
        for c in range(3):
            wts[c, i, 8:24] = ws[c]
            base[c, i, 8:24] = bs[c]
        return carry

    lax.fori_loop(0, 8, fill_own, 0)

    state[1]()

    shell = {}
    for row in (6, 7, 24, 25):
        at = across(1, row)
        shell[row] = properties(*[ext[(ch, *at)] for ch in STATE])
        for f in range(8):
            fld[(1, f, *at)] = shell[row][0][f]

    def fill_plane(plane):
        at = (plane, slice(6, 30))
        for f, value in enumerate(properties(*[ext[(ch, *at)] for ch in STATE])[0]):
            fld[(1, f, *at)] = value

    fill_plane(0)
    fill_plane(9)

    def gather(low, high):
        return jnp.where(even24, pltpu.roll(high, 127, 1), pltpu.roll(low, 1, 1))

    def spread(parts, start):
        before = pltpu.roll(parts[0], (128 - start - 14) % 128, 1)
        here = pltpu.roll(parts[1], (128 + 2 - start) % 128, 1)
        after = pltpu.roll(parts[2], (128 + 18 - start) % 128, 1)
        return jnp.where(lane24 < 2, before, jnp.where(lane24 < 18, here, after))

    parts = [[gather(zb[0, d, k, 6:30], zb[1, d, k, 6:30]) for d in range(3)] for k in range(2)]
    columns = [spread(parts[s // 8], 16 * (s % 8)) for s in range(5)]
    for f, value in enumerate(properties(*columns)[0]):
        zf[f, 6:30] = value
    for s in range(5, len(PACKED)):
        zf[3 + s, 6:30] = spread(parts[s // 8], 16 * (s % 8))

    def shift(i, carry):
        for f in range(8):
            value = fld[1, f, i, 6:30]
            edge = pltpu.roll(zf[f, 6:30], 127 - 2 * i, 1)
            fld[0, f, i, 6:30] = jnp.where(lane24 == 0, edge, pltpu.roll(value, 1, 1))
            fld[2, f, i, 6:30] = jnp.where(lane24 == 127, edge, pltpu.roll(value, 127, 1))
        for n, k in enumerate(T_ROLLED):
            at = {0: slice(6, 30), 1: slice(0, 24), -1: slice(8, 32)}[upper[k][1]]
            value = ext[TCH[k], i, at]
            edge = pltpu.roll(zf[8 + n, at], 127 - 2 * i, 1)
            if upper[k][2] > 0:
                tl[n, i, at] = jnp.where(lane24 == 0, edge, pltpu.roll(value, 1, 1))
            else:
                tl[n, i, at] = jnp.where(lane24 == 127, edge, pltpu.roll(value, 127, 1))
        return carry

    lax.fori_loop(0, 10, shift, 0)

    def equations(get, put, w, bs):
        centre = [get("fld", (1, f), 0, 0) for f in range(8)]
        p, m, mob, slope = centre[0], centre[1], centre[2:5], centre[5:8]
        mob_w = w[0] * mob[0] + w[1] * mob[1] + w[2] * mob[2]
        slope_w = w[0] * slope[0] + w[1] * slope[1] + w[2] * slope[2]
        zeros = jnp.zeros((8, 128), F32)
        sum_q, sum_t, sum_m = zeros, zeros, zeros
        sum_l = [zeros, zeros, zeros]
        for n, o in enumerate(offsets):
            dx, dy, dz = o
            if o in upper:
                t = get("ext", (TCH[upper.index(o)],), 0, 0)
            else:
                k = upper.index(minus(o))
                if dz:
                    t = get("tl", (T_ROLLED.index(k),), dx, dy)
                else:
                    t = get("ext", (TCH[k],), dx, dy)
            near = [get("fld", (dz + 1, f), dx, dy) for f in range(8)]
            t = t * near[1]
            q = t * (p - near[0])
            mw = w[0] * near[2] + w[1] * near[3] + w[2] * near[4]
            gw = w[0] * near[5] + w[1] * near[6] + w[2] * near[7]
            sum_q = sum_q + q
            sum_t = sum_t + t
            sum_m = sum_m + t * mw
            for c in range(3):
                sum_l[c] = sum_l[c] + q * near[2 + c]
            put("acoef", (n,), q * gw - t * (mob_w + mw))
        d = 1.0 + slope_w * sum_q + mob_w * sum_t + sum_m
        h = zeros
        for c in range(3):
            res = m * (bs[c] + mob[c] * sum_q + sum_l[c])
            put("resv", (c,), res)
            h = h - w[c] * res
        inv = jnp.where(m > 0, relax_weight / d, 0.0)
        put("dinv", (), inv)
        put("x0", (), inv * h)

    def assemble(i, carry):
        for a in (8, 16):
            refs = {"fld": fld, "ext": ext, "tl": tl}

            def get(name, lead, dx, dy, a=a, refs=refs):
                return refs[name][(*lead, i + 1 + dx, slice(a + dy, a + dy + 8))]

            def put(name, lead, value, a=a):
                at = slice(a, a + 8)
                if name == "x0":
                    xs[0, 1, i + 1, at] = value
                elif name == "resv":
                    res_out[lead[0], i, a - 8 : a] = value
                else:
                    {"acoef": acoef, "dinv": dinv}[name][(*lead, i, at)] = value

            at = (i, slice(a, a + 8))
            equations(get, put, [wts[(c, *at)] for c in range(3)], [base[(c, *at)] for c in range(3)])
        return carry

    lax.fori_loop(0, 8, assemble, 0)

    rest[1]()

    for row in (7, 24):
        refs = {"fld": fld, "ext": ext, "tl": tl}

        def get(name, lead, dx, dy, row=row, refs=refs):
            return refs[name][(*lead, *across(1 + dx, row + dy))]

        def put(name, lead, value, row=row):
            if name == "x0":
                xs[(0, 1, *across(1, row))] = value
            elif name != "resv":
                {"acoef": acoef, "dinv": dinv}[name][(*lead, *across(0, row))] = value

        fields, fac, sat, stored = shell[row]
        old = [get("ext", (OM + c,), 0, 0) for c in range(3)]
        equations(get, put, *weights(fields[1], get("ext", (PV,), 0, 0), old, fac, sat, stored))

    pending = []
    for n in range(3):
        wide = n != 1
        lo, hi = (7, 31) if wide else (8, 24)

        acc = jnp.zeros((hi - lo, 128), F32)
        pair = lane24[: hi - lo] // 2
        for x in range(8):
            acc = jnp.where(pair == x, pltpu.roll(xs[n, 1, x + 1, lo:hi], 2 * x + 1, 1), acc)
        px[n, lo:hi] = acc
        start, arrived, left = exchange(messages_x(n, wide), s_x.at[n], r_x.at[n])
        start()
        arrived()
        pending.append(left)
        column = spread([gather(zx[n, 0, d, 6:30], zx[n, 1, d, 6:30]) for d in range(3)], 0)

        for i in range(10):
            value = xs[n, 1, i, 6:30]
            edge = pltpu.roll(column, 127 - 2 * i, 1)
            xs[n, 0, i, 6:30] = jnp.where(lane24 == 0, edge, pltpu.roll(value, 1, 1))
            xs[n, 2, i, 6:30] = jnp.where(lane24 == 127, edge, pltpu.roll(value, 127, 1))

        def relaxed(near, coef, inv, start, value):
            total = jnp.zeros((8, 128), F32)
            for k, o in enumerate(offsets):
                total = total + coef(k) * near(*o)
            return start + (1.0 - relax_weight) * value - inv * total

        def sweep(i, carry, n=n, relaxed=relaxed):
            for a in (8, 16):
                at = slice(a, a + 8)
                value = relaxed(
                    lambda dx, dy, dz: xs[n, dz + 1, i + 1 + dx, a + dy : a + dy + 8],
                    lambda k: acoef[k, i, at],
                    dinv[i, at],
                    xs[0, 1, i + 1, at],
                    xs[n, 1, i + 1, at],
                )
                if n == 2:
                    x_out[i, a - 8 : a] = value
                else:
                    xs[n + 1, 1, i + 1, at] = value
            return carry

        lax.fori_loop(0, 8, sweep, 0)
        if n == 1:
            for row in (7, 24):
                xs[(2, 1, *across(1, row))] = relaxed(
                    lambda dx, dy, dz: xs[(1, dz + 1, *across(1 + dx, row + dy))],
                    lambda k: acoef[(k, *across(0, row))],
                    dinv[across(0, row)],
                    xs[(0, 1, *across(1, row))],
                    xs[(1, 1, *across(1, row))],
                )

    state[2]()
    rest[2]()
    for left in pending:
        left()


def body(cs, om, pv, tr, am, rg, b_tab, c_tab, v_tab):
    anywhere = pl.BlockSpec(memory_space=pltpu.HBM)
    vmem = lambda *s: pltpu.VMEM(s, F32)
    dma = lambda *s: pltpu.SemaphoreType.DMA(s)
    return pl.pallas_call(
        kernel,
        out_shape=(
            jax.ShapeDtypeStruct((3, 8, 16, 128), F32),
            jax.ShapeDtypeStruct((8, 16, 128), F32),
        ),
        in_specs=[anywhere] * 9,
        out_specs=(pl.BlockSpec(memory_space=pltpu.VMEM),) * 2,
        scratch_shapes=[
            *[pltpu.SMEM((3, 8), F32)] * 3,
            vmem(NCH, NP, NR, 128),
            pltpu.VMEM((2, 8, 16, 128), jnp.int32),
            vmem(3, 8, NP, NR, 128),
            vmem(len(T_ROLLED), NP, NR, 128),
            vmem(3, 8, NR, 128),
            vmem(3, 8, NR, 128),
            vmem(26, 8, NR, 128),
            vmem(8, NR, 128),
            vmem(3, 3, NP, NR, 128),
            vmem(3, NR, 128),
            vmem(3, 2, 3, NR, 128),
            vmem(2, NR, 128),
            vmem(2, 3, 2, NR, 128),
            vmem(8 + len(T_ROLLED), NR, 128),
            dma(12),
            dma(28),
            dma(28),
            dma(3),
            dma(3),
            dma(3, 26),
            dma(3, 26),
        ],
        compiler_params=pltpu.CompilerParams(
            collective_id=0, has_side_effects=True, vmem_limit_bytes=60 * 1024 * 1024
        ),
    )(cs, om, pv, tr, am, rg, b_tab, c_tab, v_tab)


def solution(mesh):
    four = P(None, "gx", "gy", "gz")
    three = P("gx", "gy", "gz")
    return jax.shard_map(
        body,
        mesh=mesh,
        in_specs=(four, four, three, four, three, three, P(), P(), P()),
        out_specs=(four, three),
        check_vma=False,
    )
```

time: 163 us -> 45.1 us (0.28)
  starting transfers between devices: 66.9 us -> 0 us
  waiting for transfers between devices: 53.8 us -> 0 us
  Pallas kernels: 0 us -> 42 us
  other arithmetic: 23.3 us -> 0 us
  local copies, waits for them, and re-layouts: 16.3 us -> 2.28 us
    ppermute x24 -> x0, starting transfers between devices: 66.9 us -> none  [the longest x12 41.8 us: extended(): lax.ppermute(tail, axis, [(i, (i + 1) % count) for i in range(ends)])]
    ppermute x24 -> x0, waiting for transfers between devices: 53.8 us -> none  [the longest x12 48.9 us: extended(): lax.ppermute(head, axis, [((i + 1) % count, i) for i in range(ends)])]
    pallas_call x0 -> x1, Pallas kernels: none -> 42 us  [body(): pl.pallas_call(kernel, out_shape=(jax.ShapeDtypeStruct((3, 8, 16, 128), F...]
    concatenate x11 -> x0, other arithmetic: 8.74 us -> none  [extended(): jnp.concatenate([lax.ppermute(tail, axis, [(i, (i + 1) % count) for i in...]
    ppermute x2 -> x0, local copies, waits for them, and re-layouts: 5.55 us -> none  [the longest x1 3.45 us: extended(): lax.ppermute(head, axis, [((i + 1) % count, i) for i in range(ends)])]
    reduce_sum x9 -> x0, other arithmetic: 5.5 us -> none  [the longest x8 5.3 us: assemble(): jnp.sum(weights * (0.5 * window(slope_all, offset) * press_drop - mobilit...]
    slice x9 -> x0, local copies, waits for them, and re-layouts: 4.26 us -> none  [the longest x7 2.36 us: extended(): lax.slice_in_dim(cells, cells.shape[dim] - width, cells.shape[dim], axis=...]
    unnamed x64 -> x4, local copies, waits for them, and re-layouts: 6.45 us -> 2.28 us
  transfers between devices with their start and end apart: 24 -> 0, of which waited for: 16 -> 0; matrix products, arithmetic and copies ran while one was open for 3% -> 0% of each run, Pallas kernels for 0% -> 0%
where the time goes in v1:
time: 45.1 us; the launch traced here: 45 us
  Pallas kernels  42 us (93%)
  local copies, waits for them, and re-layouts  2.28 us (5%)
  between operations  0.65 us (1%)
    pallas_call x1, Pallas kernels, body(): pl.pallas_call(kernel, out_shape=(jax.ShapeDtypeStruct((3, 8, 16, 128), F...  42 us
    unnamed x4, local copies, waits for them, and re-layouts  2.28 us

profile of v1, /device:TPU:185, one launch (start us, length us, event | category | flops | bytes accessed | tf_op | source)
XLA Modules:
  0.0 45.0 jit_solution(240521702065732775)
XLA Ops:
  0.6 42.0 %shard_map.104 = (f32[3,8,16,128]{3,2,1,0:T(8,128)}, f32[8,16,128]{2,1,0:T(8,128)}) custom-call(f32[3,8,16,128]{3,2,1,0:T(8,128)} %cs.1, f32[3,8,16,128]{3,2,1,0:T(8,128)} %om.1, f32[8,16,128]{2,1,0:T(8,128)} %pv.1, f32[13,8,16,128]{3,2,1,0:T(8,128)} %tr.1, s32[8,16,128]{2,1,0:T(8,128)} %am.1, s32[8,16,128]{2,1,0:T(8,128)} %rg.1, f32[3,8]{1,0:T(4,128)} %b_hbm.1, ...), custom_call_target="tpu_custom_call" | custom-call | tf_op jit(solution)/shard_map/pallas_call | solution.py:473
  42.7 0.0 copy-start
  42.7 1.6 %copy.13 = f32[3,8,16,128]{3,2,1,0:T(8,128)} copy(f32[3,8,16,128]{3,2,1,0:T(8,128)} %get-tuple-element.4) | data formatting | bytes 393216
  44.3 0.0 copy-done
  44.3 0.6 %copy.14 = f32[8,16,128]{2,1,0:T(8,128)} copy(f32[8,16,128]{2,1,0:T(8,128)S(1)} %copy-done) | data formatting | bytes 131072
Async XLA Ops:
  42.7 1.7 %copy-start = (f32[8,16,128]{2,1,0:T(8,128)S(1)}, f32[8,16,128]{2,1,0:T(8,128)}, u32[]{:S(2)}) copy-start(f32[8,16,128]{2,1,0:T(8,128)} %get-tuple-element.5) | copy-start | bytes 196612

commit v2 on v1

--- a/solution.py
+++ b/solution.py
@@ -40,8 +40,8 @@
 def kernel(
     cs, om, pv, tr, am, rg, b_hbm, c_hbm, v_hbm,
     res_out, x_out,
-    b_tab, c_tab, v_tab, ext, ints, fld, tl, wts, base, acoef, dinv, xs, px, zx, pk, zb, zf,
-    in_sem, s_state, r_state, s_rest, r_rest, s_x, r_x,
+    b_tab, c_tab, v_tab, ext, ints, fld, tl, wts, base, acoef, dinv, xs, px, zx, pk, zb, zf, resv, xv,
+    in_sem, out_sem, s_state, r_state, s_rest, r_rest, s_x, r_x,
 ):
     me = [lax.axis_index(a) for a in AXES]
     dims = [lax.axis_size(a) for a in AXES]
@@ -122,22 +122,6 @@
         return carry
 
     lax.fori_loop(0, 8, convert, 0)
-
-    lane16 = lax.broadcasted_iota(jnp.int32, (16, 128), 1)
-    lane24 = lax.broadcasted_iota(jnp.int32, (24, 128), 1)
-    even24 = lane24 % 2 == 0
-
-    def pack(x, accs):
-        accs = list(accs)
-        for s, ch in enumerate(PACKED):
-            to = 16 * (s % 8) + 2 * x
-            moved = pltpu.roll(ext[ch, x + 1, 8:24], to + 1, 1)
-            accs[s // 8] = jnp.where((lane16 == to) | (lane16 == to + 1), moved, accs[s // 8])
-        return tuple(accs)
-
-    packed = lax.fori_loop(0, 8, pack, (jnp.zeros((16, 128), F32),) * 2)
-    for k in range(2):
-        pk[k, 8:24] = packed[k]
 
     peers = 1
     for i in range(3):
@@ -176,7 +160,7 @@
     def messages_x(n, wide):
         x = xs.at[n, 1]
         found = []
-        for o in offsets:
+        for o in sorted(offsets, key=lambda o: (-abs(o[1]), -abs(o[0]) - abs(o[2]))):
             dx, dy, dz = o
             if wide and dy:
                 continue
@@ -207,9 +191,10 @@
             for i, (o, a, b) in enumerate(found)
         ]
 
-        def start():
+        def start(along_z=None):
             for o, c in found:
-                pl.when(present(o))(c.start)
+                if along_z is None or along_z == (o[2] != 0):
+                    pl.when(present(o))(c.start)
 
         def arrived():
             for o, c in found:
@@ -223,7 +208,24 @@
 
     state = exchange(messages_state(), s_state, r_state)
     rest = exchange(messages_rest(), s_rest, r_rest)
-    state[0]()
+    state[0](False)
+    lane16 = lax.broadcasted_iota(jnp.int32, (16, 128), 1)
+    lane24 = lax.broadcasted_iota(jnp.int32, (24, 128), 1)
+    even24 = lane24 % 2 == 0
+
+    def pack(x, accs):
+        accs = list(accs)
+        for s, ch in enumerate(PACKED):
+            to = 16 * (s % 8) + 2 * x
+            moved = pltpu.roll(ext[ch, x + 1, 8:24], to + 1, 1)
+            accs[s // 8] = jnp.where((lane16 == to) | (lane16 == to + 1), moved, accs[s // 8])
+        return tuple(accs)
+
+    packed = lax.fori_loop(0, 8, pack, (jnp.zeros((16, 128), F32),) * 2, unroll=2)
+    for k in range(2):
+        pk[k, 8:24] = packed[k]
+
+    state[0](True)
     rest[0]()
 
     tables = [[[t[c, k] for k in range(8)] for c in range(3)] for t in (b_tab, c_tab, v_tab)]
@@ -255,6 +257,12 @@
     def across(plane, row):
         return (slice(plane, plane + 8), row)
 
+    flat = lambda ref, n: ref.reshape(*ref.shape[:-3], n * NR, 128)
+    fld_f, tl_f, acoef_f, dinv_f = flat(fld, NP), flat(tl, NP), flat(acoef, 8), flat(dinv, 8)
+
+    def strided(plane, row):
+        return (pl.ds(plane * NR + row, 8, stride=NR), slice(None))
+
     def weights(m, vol, old, fac, sat, stored):
         scale = 1.0 / jnp.where(m > 0, vol * stored, 1.0)
         return [scale / f for f in fac], [vol * f * v - o for f, v, o in zip(fac, sat, old)]
@@ -282,7 +290,7 @@
         at = across(1, row)
         shell[row] = properties(*[ext[(ch, *at)] for ch in STATE])
         for f in range(8):
-            fld[(1, f, *at)] = shell[row][0][f]
+            fld_f[(1, f, *strided(1, row))] = shell[row][0][f]
 
     def fill_plane(plane):
         at = (plane, slice(6, 30))
@@ -324,7 +332,7 @@
                 tl[n, i, at] = jnp.where(lane24 == 127, edge, pltpu.roll(value, 127, 1))
         return carry
 
-    lax.fori_loop(0, 10, shift, 0)
+    lax.fori_loop(0, 10, shift, 0, unroll=2)
 
     def equations(get, put, w, bs):
         centre = [get("fld", (1, f), 0, 0) for f in range(8)]
@@ -377,7 +385,7 @@
                 if name == "x0":
                     xs[0, 1, i + 1, at] = value
                 elif name == "resv":
-                    res_out[lead[0], i, a - 8 : a] = value
+                    resv[lead[0], i, a - 8 : a] = value
                 else:
                     {"acoef": acoef, "dinv": dinv}[name][(*lead, i, at)] = value
 
@@ -386,20 +394,22 @@
         return carry
 
     lax.fori_loop(0, 8, assemble, 0)
+    out_copies = [pltpu.make_async_copy(resv, res_out, out_sem.at[0]), pltpu.make_async_copy(xv, x_out, out_sem.at[1])]
+    out_copies[0].start()
 
     rest[1]()
 
     for row in (7, 24):
-        refs = {"fld": fld, "ext": ext, "tl": tl}
-
-        def get(name, lead, dx, dy, row=row, refs=refs):
-            return refs[name][(*lead, *across(1 + dx, row + dy))]
+        def get(name, lead, dx, dy, row=row):
+            if name == "ext":
+                return ext[(*lead, *across(1 + dx, row + dy))]
+            return {"fld": fld_f, "tl": tl_f}[name][(*lead, *strided(1 + dx, row + dy))]
 
         def put(name, lead, value, row=row):
             if name == "x0":
                 xs[(0, 1, *across(1, row))] = value
             elif name != "resv":
-                {"acoef": acoef, "dinv": dinv}[name][(*lead, *across(0, row))] = value
+                {"acoef": acoef_f, "dinv": dinv_f}[name][(*lead, *strided(0, row))] = value
 
         fields, fac, sat, stored = shell[row]
         old = [get("ext", (OM + c,), 0, 0) for c in range(3)]
@@ -444,26 +454,29 @@
                     xs[n, 1, i + 1, at],
                 )
                 if n == 2:
-                    x_out[i, a - 8 : a] = value
+                    xv[i, a - 8 : a] = value
                 else:
                     xs[n + 1, 1, i + 1, at] = value
             return carry
 
-        lax.fori_loop(0, 8, sweep, 0)
+        lax.fori_loop(0, 8, sweep, 0, unroll=4)
         if n == 1:
             for row in (7, 24):
                 xs[(2, 1, *across(1, row))] = relaxed(
                     lambda dx, dy, dz: xs[(1, dz + 1, *across(1 + dx, row + dy))],
-                    lambda k: acoef[(k, *across(0, row))],
-                    dinv[across(0, row)],
+                    lambda k: acoef_f[(k, *strided(0, row))],
+                    dinv_f[strided(0, row)],
                     xs[(0, 1, *across(1, row))],
                     xs[(1, 1, *across(1, row))],
                 )
 
+    out_copies[1].start()
     state[2]()
     rest[2]()
     for left in pending:
         left()
+    for c in out_copies:
+        c.wait()
 
 
 def body(cs, om, pv, tr, am, rg, b_tab, c_tab, v_tab):
@@ -477,7 +490,7 @@
             jax.ShapeDtypeStruct((8, 16, 128), F32),
         ),
         in_specs=[anywhere] * 9,
-        out_specs=(pl.BlockSpec(memory_space=pltpu.VMEM),) * 2,
+        out_specs=(anywhere,) * 2,
         scratch_shapes=[
             *[pltpu.SMEM((3, 8), F32)] * 3,
             vmem(NCH, NP, NR, 128),
@@ -494,7 +507,10 @@
             vmem(2, NR, 128),
             vmem(2, 3, 2, NR, 128),
             vmem(8 + len(T_ROLLED), NR, 128),
+            vmem(3, 8, 16, 128),
+            vmem(8, 16, 128),
             dma(12),
+            dma(2),
             dma(28),
             dma(28),
             dma(3),

time: 45.1 us -> 44.1 us (0.978)
  Pallas kernels: 42 us -> 41 us
    pallas_call x1, Pallas kernels: 42 us -> 41 us  [body(): pl.pallas_call(kernel, out_shape=(jax.ShapeDtypeStruct((3, 8, 16, 128), F...]
where the time goes in v2:
time: 44.1 us; the launch traced here: 44 us
  Pallas kernels  41 us (93%)
  local copies, waits for them, and re-layouts  2.28 us (5%)
  between operations  0.65 us (1%)
    pallas_call x1, Pallas kernels, body(): pl.pallas_call(kernel, out_shape=(jax.ShapeDtypeStruct((3, 8, 16, 128), F...  41 us
    unnamed x4, local copies, waits for them, and re-layouts  2.28 us

profile of v2, /device:TPU:185, one launch (start us, length us, event | category | flops | bytes accessed | tf_op | source)
XLA Modules:
  0.0 44.0 jit_solution(2089982470751070878)
XLA Ops:
  0.6 41.0 %shard_map.104 = (f32[3,8,16,128]{3,2,1,0:T(8,128)}, f32[8,16,128]{2,1,0:T(8,128)}) custom-call(f32[3,8,16,128]{3,2,1,0:T(8,128)} %cs.1, f32[3,8,16,128]{3,2,1,0:T(8,128)} %om.1, f32[8,16,128]{2,1,0:T(8,128)} %pv.1, f32[13,8,16,128]{3,2,1,0:T(8,128)} %tr.1, s32[8,16,128]{2,1,0:T(8,128)} %am.1, s32[8,16,128]{2,1,0:T(8,128)} %rg.1, f32[3,8]{1,0:T(4,128)} %b_hbm.1, ...), custom_call_target="tpu_custom_call" | custom-call | tf_op jit(solution)/shard_map/pallas_call | solution.py:486
  41.7 0.0 copy-start
  41.7 1.6 %copy.13 = f32[3,8,16,128]{3,2,1,0:T(8,128)} copy(f32[3,8,16,128]{3,2,1,0:T(8,128)} %get-tuple-element.4) | data formatting | bytes 393216
  43.3 0.0 copy-done
  43.4 0.6 %copy.14 = f32[8,16,128]{2,1,0:T(8,128)} copy(f32[8,16,128]{2,1,0:T(8,128)S(1)} %copy-done) | data formatting | bytes 131072
Async XLA Ops:
  41.7 1.7 %copy-start = (f32[8,16,128]{2,1,0:T(8,128)S(1)}, f32[8,16,128]{2,1,0:T(8,128)}, u32[]{:S(2)}) copy-start(f32[8,16,128]{2,1,0:T(8,128)} %get-tuple-element.5) | copy-start | bytes 196612

commit v3 on v2

--- a/solution.py
+++ b/solution.py
@@ -221,7 +221,7 @@
             accs[s // 8] = jnp.where((lane16 == to) | (lane16 == to + 1), moved, accs[s // 8])
         return tuple(accs)
 
-    packed = lax.fori_loop(0, 8, pack, (jnp.zeros((16, 128), F32),) * 2, unroll=2)
+    packed = lax.fori_loop(0, 8, pack, (jnp.zeros((16, 128), F32),) * 2, unroll=4)
     for k in range(2):
         pk[k, 8:24] = packed[k]
 
@@ -332,7 +332,7 @@
                 tl[n, i, at] = jnp.where(lane24 == 127, edge, pltpu.roll(value, 127, 1))
         return carry
 
-    lax.fori_loop(0, 10, shift, 0, unroll=2)
+    lax.fori_loop(0, 10, shift, 0, unroll=5)
 
     def equations(get, put, w, bs):
         centre = [get("fld", (1, f), 0, 0) for f in range(8)]
@@ -393,7 +393,7 @@
             equations(get, put, [wts[(c, *at)] for c in range(3)], [base[(c, *at)] for c in range(3)])
         return carry
 
-    lax.fori_loop(0, 8, assemble, 0)
+    lax.fori_loop(0, 8, assemble, 0, unroll=2)
     out_copies = [pltpu.make_async_copy(resv, res_out, out_sem.at[0]), pltpu.make_async_copy(xv, x_out, out_sem.at[1])]
     out_copies[0].start()
 

time: 44.1 us -> 43.9 us (level)
  no operation moved by 1% of the time
where the time goes in v3:
time: 43.9 us; the launch traced here: 43.7 us
  Pallas kernels  40.8 us (93%)
  local copies, waits for them, and re-layouts  2.28 us (5%)
  between operations  0.65 us (1%)
    pallas_call x1, Pallas kernels, body(): pl.pallas_call(kernel, out_shape=(jax.ShapeDtypeStruct((3, 8, 16, 128), F...  40.8 us
    unnamed x4, local copies, waits for them, and re-layouts  2.28 us

profile of v3, /device:TPU:185, one launch (start us, length us, event | category | flops | bytes accessed | tf_op | source)
XLA Modules:
  0.0 43.7 jit_solution(16478531983140130464)
XLA Ops:
  0.6 40.8 %shard_map.104 = (f32[3,8,16,128]{3,2,1,0:T(8,128)}, f32[8,16,128]{2,1,0:T(8,128)}) custom-call(f32[3,8,16,128]{3,2,1,0:T(8,128)} %cs.1, f32[3,8,16,128]{3,2,1,0:T(8,128)} %om.1, f32[8,16,128]{2,1,0:T(8,128)} %pv.1, f32[13,8,16,128]{3,2,1,0:T(8,128)} %tr.1, s32[8,16,128]{2,1,0:T(8,128)} %am.1, s32[8,16,128]{2,1,0:T(8,128)} %rg.1, f32[3,8]{1,0:T(4,128)} %b_hbm.1, ...), custom_call_target="tpu_custom_call" | custom-call | tf_op jit(solution)/shard_map/pallas_call | solution.py:486
  41.4 0.0 copy-start
  41.4 1.6 %copy.13 = f32[3,8,16,128]{3,2,1,0:T(8,128)} copy(f32[3,8,16,128]{3,2,1,0:T(8,128)} %get-tuple-element.4) | data formatting | bytes 393216
  43.1 0.0 copy-done
  43.1 0.6 %copy.14 = f32[8,16,128]{2,1,0:T(8,128)} copy(f32[8,16,128]{2,1,0:T(8,128)S(1)} %copy-done) | data formatting | bytes 131072
Async XLA Ops:
  41.4 1.7 %copy-start = (f32[8,16,128]{2,1,0:T(8,128)S(1)}, f32[8,16,128]{2,1,0:T(8,128)}, u32[]{:S(2)}) copy-start(f32[8,16,128]{2,1,0:T(8,128)} %get-tuple-element.5) | copy-start | bytes 196612
